TPU v7x, 32 devices: a whole 2x2x4 slice. The times are simulated.
32 devices in a mesh: groups: 2 (over x), tensor: 16 (over z, y, core).
Axes of the slice: x: 2, y: 2, z: 4, core: 2. Of those that a mesh axis runs over, the one named last changes fastest.
Arguments:
- tokens: bfloat16 [512, 8192], P(('groups', 'tensor')), parts along dimension 0, may hold values from -6 to 6
- gate_weight: bfloat16 [8192, 16384], P(None, 'tensor'), may hold values from -0.0625 to 0.0625
- up_weight: bfloat16 [8192, 16384], P(None, 'tensor'), may hold values from -0.0625 to 0.0625
- adapter_down_weight: bfloat16 [32, 64, 8192], P(('groups', 'tensor')), parts along dimension 0, may hold values from -0.0625 to 0.0625
- adapter_up_weight: bfloat16 [32, 64, 16384], P(('groups', 'tensor')), parts along dimension 0, may hold values from -0.75 to 0.75
- row_adapter: int32 [512], P('groups'), parts along dimension 0, may hold values from 0 to 15, as said below
- sorted_rows: int32 [512], P('groups'), parts along dimension 0, may hold values from 0 to 255, as said below
- segment_count: int32 [32], P('groups'), parts along dimension 0, may hold values from 1 to 64, as said below
Outputs:
- hidden: bfloat16 [512, 16384], P('groups', 'tensor'), parts along dimension 0
There are 2 independent parts, one for each index of `groups`. A program takes and returns all parts, laid end to end along the dimension named above; an argument that names none is the same for every part. Nothing has to cross between parts.
Inputs may be any that keep to these rules, and one draw needn't show every extreme that they name: Row r uses adapter row_adapter[r]; adapter j is used by segment_count[j] rows. `sorted_rows`: a permutation of the rows; the rows of adapter j stand at positions seg_start[j] to seg_start[j] + segment_count[j] - 1. `segment_count`: the counts sum to 256; some adapter has exactly 64 rows.
All inputs are finite; a program needn't handle non-finite values.
Results may differ from a plain program's by a relative error of at most 0.0036.
Values may be sent and summed in bfloat16 or wider, within the bound.
No kernel may reach another device: no remote copies, remote signals or barrier semaphores. Data moves between devices by JAX's collectives and lax.ppermute only.
A program may use at most 128 MiB of HBM per device.

v0:
```python
import functools

import jax
import jax.numpy as jnp
from jax import lax
from jax.experimental import pallas as pl
from jax.experimental.pallas import tpu as pltpu
from jax.sharding import PartitionSpec as P

ADAPTER_SCALE = 0.5
ROWS_PER_LIMIT = 64
SLOT_SIZES = (80, 96)
CORES = 2
MIB = 1024 * 1024


def chip_ring(chips):
    return list(range(0, chips, 2)) + list(range(chips - 1, 0, -2))


def ring_chip(me, chips, distance):
    chip = me // CORES
    place = jnp.where(chip % 2 == 0, chip // 2, chips // 2 + (chips - 1 - chip) // 2)
    place = (place + distance + chips) % chips
    return jnp.where(place < chips // 2, 2 * place, chips - 1 - 2 * (place - chips // 2))


def ring_gather(block, axis, beside):
    size = lax.axis_size(axis)
    chips = size // CORES
    ring = chip_ring(chips)

    def moved(value, shift):
        pairs = [
            (ring[p] * CORES + k, ring[(p + shift) % chips] * CORES + k)
            for p in range(chips)
            for k in range(CORES)
        ]
        return lax.ppermute(value, axis, pairs)

    half = block.shape[1] // 2
    far = chips // 2
    halves = block[:, :half], block[:, half:]
    columns = (0, half), (half, 0)
    held = [halves, halves[::-1]]
    pieces = [(block, 0, 0)]
    for step in range(1, far + 1):
        for chain in range(1 if step == far else 2):
            right, left = held[chain]
            held[chain] = moved(right, 1), moved(left, -1)
            for value, column, distance in zip(held[chain], columns[chain], (-step, step)):
                pieces.append((value, column, distance))
        held = beside(step, held)
    return pieces


ANY_SPEC = pl.BlockSpec(memory_space=pl.ANY)


def in_hbm(values):
    return [pltpu.with_memory_space_constraint(value, pltpu.HBM) for value in values]


def run_copies(copies):
    for copy in copies:
        copy.start()
    for copy in copies:
        copy.wait()


def make_plan(sizes, counts, sorted_ref, held_ref, choice_ref):
    chips, most = held_ref.shape
    rows = sorted_ref.shape[1]
    adapters = counts[0].shape[0] // chips

    def total(group, chip):
        return functools.reduce(jnp.add, [counts[group][chip * adapters + a] for a in range(adapters)])

    listed = jnp.broadcast_to(sorted_ref[...], (8, rows))
    slot = lax.broadcasted_iota(jnp.int32, (8, most), 1)
    start = jnp.int32(0)
    for chip in range(chips):
        turned = pltpu.roll(listed, (rows - start) % rows, 1)
        held_ref[chip : chip + 1, :] = jnp.where(slot < total(0, chip), turned[:, :most], -1)[0:1]
        start += total(0, chip)
    largest = functools.reduce(
        jnp.maximum, [total(group, chip) for group in range(len(counts)) for chip in range(chips)]
    )
    choice_ref[0] = functools.reduce(jnp.add, [(largest > size).astype(jnp.int32) for size in sizes[:-1]])


def down_copies(core, own_down_ref, other_down_ref, down_vmem, sems):
    ranks = own_down_ref.shape[0]
    return [
        pltpu.make_async_copy(ref, down_vmem.at[pl.ds(pl.multiple_of(where * ranks, ranks), ranks)], sems.at[i])
        for i, (ref, where) in enumerate(((own_down_ref, core), (other_down_ref, 1 - core)))
    ]


def shrink_near_kernel(sizes, places, groups, me, *refs):
    counts, refs = refs[:groups], refs[groups:]
    sorted_ref, own_down_ref, other_down_ref = refs[:3]
    refs = refs[3:]
    piece_refs = refs[: len(places)]
    tokens_ref, shrunk_ref, held_ref, choice_ref, tokens_vmem, down_vmem, sems = refs[len(places) :]
    chips = held_ref.shape[0]
    copies = down_copies(me[0] % CORES, own_down_ref, other_down_ref, down_vmem, sems)
    for ref, (column, distance) in zip(piece_refs, places):
        rows, width = ref.shape
        start = pl.multiple_of(ring_chip(me[0], chips, distance) * rows, rows)
        copies.append(
            pltpu.make_async_copy(
                ref, tokens_vmem.at[pl.ds(start, rows), pl.ds(column, width)], sems.at[len(copies)]
            )
        )
    for copy in copies:
        copy.start()
    make_plan(sizes, counts, sorted_ref, held_ref, choice_ref)
    for copy in copies:
        copy.wait()
    out_copy = pltpu.make_async_copy(tokens_vmem, tokens_ref, sems.at[len(copies)])
    out_copy.start()
    shrunk_ref[...] = lax.dot_general(
        tokens_vmem[...], down_vmem[...], (((1,), (1,)), ((), ())), preferred_element_type=jnp.float32
    ).astype(shrunk_ref.dtype)
    out_copy.wait()


def shrink_far_kernel(me, tokens_in, shrunk_in, own_down_ref, other_down_ref, *refs):
    piece_refs = refs[:2]
    tokens_ref, shrunk_ref, far_vmem, down_vmem, sems = refs[2:]
    rows, width = far_vmem.shape
    chips = tokens_in.shape[0] // rows
    start = pl.multiple_of(ring_chip(me[0], chips, chips // 2) * rows, rows)
    copies = down_copies(me[0] % CORES, own_down_ref, other_down_ref, down_vmem, sems)
    half = width // 2
    for i, ref in enumerate(piece_refs):
        copies.append(pltpu.make_async_copy(ref, far_vmem.at[:, pl.ds(i * half, half)], sems.at[2 + i]))
    run_copies(copies)
    out_copy = pltpu.make_async_copy(far_vmem, tokens_ref.at[pl.ds(start, rows)], sems.at[4])
    out_copy.start()
    shrunk_ref[...] = shrunk_in[...]
    shrunk_ref[pl.ds(start, rows), :] = lax.dot_general(
        far_vmem[...], down_vmem[...], (((1,), (1,)), ((), ())), preferred_element_type=jnp.float32
    ).astype(shrunk_ref.dtype)
    out_copy.wait()


def shrink(me, counts, sorted_rows, pieces, own_down, other_down, sizes):
    ranks, width = own_down.shape
    rows_all = sorted_rows.shape[0]
    rows = rows_all // CORES
    values = [value for value, _, _ in pieces]
    near = values[:-2]
    block = values[0].shape[0]
    tokens_shape = pltpu.HBM((rows, width), jnp.bfloat16)
    shrunk_shape = jax.ShapeDtypeStruct((rows, CORES * ranks), jnp.bfloat16)
    held_shape = jax.ShapeDtypeStruct((rows // block, sizes[-1]), jnp.int32)

    def whole(shape):
        return pl.BlockSpec(shape, lambda i, *_: (0, 0))

    down_vmem = pltpu.VMEM((CORES * ranks, width), jnp.bfloat16)
    downs = in_hbm([own_down, other_down])
    tokens, shrunk, held, choice = pl.pallas_call(
        functools.partial(shrink_near_kernel, sizes, [place[1:] for place in pieces[:-2]], len(counts)),
        grid_spec=pltpu.PrefetchScalarGridSpec(
            num_scalar_prefetch=1 + len(counts),
            grid=(1,),
            in_specs=[whole((1, rows_all))] + [ANY_SPEC] * (2 + len(near)),
            out_specs=[
                ANY_SPEC,
                whole(shrunk_shape.shape),
                whole(held_shape.shape),
                pl.BlockSpec(memory_space=pltpu.SMEM),
            ],
            scratch_shapes=[
                pltpu.VMEM((rows, width), jnp.bfloat16),
                down_vmem,
                pltpu.SemaphoreType.DMA((3 + len(near),)),
            ],
        ),
        out_shape=[tokens_shape, shrunk_shape, held_shape, jax.ShapeDtypeStruct((1,), jnp.int32)],
        compiler_params=pltpu.CompilerParams(vmem_limit_bytes=rows * width * 2 + 16 * MIB),
        name="shrink_near",
    )(me, *counts, sorted_rows.reshape(1, rows_all), *downs, *in_hbm(near[:1]), *near[1:])
    tokens, shrunk = pl.pallas_call(
        shrink_far_kernel,
        grid_spec=pltpu.PrefetchScalarGridSpec(
            num_scalar_prefetch=1,
            grid=(1,),
            in_specs=[ANY_SPEC, whole(shrunk_shape.shape)] + [ANY_SPEC] * 4,
            out_specs=[ANY_SPEC, whole(shrunk_shape.shape)],
            scratch_shapes=[
                pltpu.VMEM((block, width), jnp.bfloat16),
                down_vmem,
                pltpu.SemaphoreType.DMA((5,)),
            ],
        ),
        out_shape=[tokens_shape, shrunk_shape],
        input_output_aliases={1: 0},
        compiler_params=pltpu.CompilerParams(vmem_limit_bytes=16 * MIB),
        name="shrink_far",
    )(me, *in_hbm([tokens]), shrunk, *downs, *values[-2:])
    return tokens, shrunk, held, choice


def expand_kernel(block, counts, me, held_ref, own_ref, other_ref, keep_ref, got_ref, out_ref, maps_vmem, out_vmem, sems):
    chips, slots, units = out_vmem.shape
    most = held_ref.shape[1]
    ranks = keep_ref.shape[0]
    adapters = counts.shape[0] // chips
    chip = me[0] // CORES
    core = me[0] % CORES
    copies = []
    for c in range(chips):
        start = pl.multiple_of((c * CORES + core) * units, units)
        for ref, where in ((keep_ref, core), (got_ref, 1 - core)):
            copies.append(
                pltpu.make_async_copy(
                    ref.at[:, pl.ds(start, units)],
                    maps_vmem.at[c, pl.ds(pl.multiple_of(where * ranks, ranks), ranks)],
                    sems.at[len(copies)],
                )
            )
    for copy in copies:
        copy.start()

    wanted = held_ref[pl.ds(chip, 1), :]
    index = lax.broadcasted_iota(jnp.int32, (own_ref.shape[0], most), 0)
    row = index // block * (CORES * block) + index % block
    picked = jnp.zeros((most, own_ref.shape[1]), jnp.float32)
    for ref, where in ((own_ref, core), (other_ref, 1 - core)):
        hit = (row + where * block == wanted).astype(jnp.float32).astype(jnp.bfloat16)
        picked += lax.dot_general(hit, ref[...], (((0,), (0,)), ((), ())), preferred_element_type=jnp.float32)
    slot = lax.broadcasted_iota(jnp.int32, picked.shape, 0)
    adapter = lax.broadcasted_iota(jnp.int32, picked.shape, 1) // (picked.shape[1] // adapters)
    mine = jnp.zeros(picked.shape, jnp.int32)
    first = jnp.int32(0)
    for a in range(adapters):
        end = first + counts[chip * adapters + a]
        mine += ((adapter == a) & (slot >= first) & (slot < end)).astype(jnp.int32)
        first = end
    shrunk = jnp.where(mine > 0, picked, 0.0).astype(jnp.bfloat16)[:slots]

    out_copies = []
    for c in range(chips):
        copies[2 * c].wait()
        copies[2 * c + 1].wait()
        product = jnp.dot(shrunk, maps_vmem[c], preferred_element_type=jnp.float32)
        out_vmem[c] = (ADAPTER_SCALE * product).astype(out_vmem.dtype)
        out_copies.append(pltpu.make_async_copy(out_vmem.at[c], out_ref.at[c], sems.at[2 * chips + c]))
        out_copies[-1].start()
    for copy in out_copies:
        copy.wait()


def expand(counts, me, held, own_shrunk, other_shrunk, keep, got, slots, block):
    ranks, columns = keep.shape
    chips, most = held.shape
    units = columns // chips // CORES
    rows, ranks_all = own_shrunk.shape
    shrunk_spec = pl.BlockSpec((rows, ranks_all), lambda i, s, t: (0, 0))
    return pl.pallas_call(
        functools.partial(expand_kernel, block),
        grid_spec=pltpu.PrefetchScalarGridSpec(
            num_scalar_prefetch=2,
            grid=(1,),
            in_specs=[
                pl.BlockSpec((chips, most), lambda i, s, t: (0, 0)),
                shrunk_spec,
                shrunk_spec,
                ANY_SPEC,
                ANY_SPEC,
            ],
            out_specs=ANY_SPEC,
            scratch_shapes=[
                pltpu.VMEM((chips, ranks_all, units), jnp.bfloat16),
                pltpu.VMEM((chips, slots, units), jnp.bfloat16),
                pltpu.SemaphoreType.DMA((3 * chips,)),
            ],
        ),
        out_shape=pltpu.HBM((chips, slots, units), jnp.bfloat16),
        compiler_params=pltpu.CompilerParams(vmem_limit_bytes=16 * MIB),
        cost_estimate=pl.CostEstimate(
            flops=2 * slots * ranks_all * chips * units,
            bytes_accessed=2 * (slots + ranks_all) * chips * units,
            transcendentals=0,
        ),
        name="expand",
    )(counts, me, held, own_shrunk, other_shrunk, *in_hbm([keep, got]))


def project_kernel(block, me, gate_weight_ref, up_weight_ref, own_ref, other_ref, gate_ref, up_ref, tokens_vmem, sems):
    depth = gate_weight_ref.shape[0]
    core = me[0] % CORES
    k = pl.program_id(0)

    @pl.when(k == 0)
    def _():
        copies = []
        for ref, where in ((own_ref, core), (other_ref, 1 - core)):
            for chip in range(ref.shape[0] // block):
                start = pl.multiple_of((chip * CORES + where) * block, block)
                copies.append(
                    pltpu.make_async_copy(
                        ref.at[pl.ds(chip * block, block)], tokens_vmem.at[pl.ds(start, block)], sems.at[len(copies)]
                    )
                )
        run_copies(copies)
        gate_ref[...] = jnp.zeros_like(gate_ref)
        up_ref[...] = jnp.zeros_like(up_ref)

    tokens = tokens_vmem[:, pl.ds(pl.multiple_of(k * depth, depth), depth)]
    gate_ref[...] += jnp.dot(tokens, gate_weight_ref[...], preferred_element_type=jnp.float32)
    up_ref[...] += jnp.dot(tokens, up_weight_ref[...], preferred_element_type=jnp.float32)

    @pl.when(k == pl.num_programs(0) - 1)
    def _():
        gate = gate_ref[...]
        gate_ref[...] = gate / (1.0 + jnp.exp(-gate))


def project(me, own, other, gate_weight, up_weight, block):
    width, units = gate_weight.shape
    rows = CORES * own.shape[0]
    depth = min(1024, width)
    weight_spec = pl.BlockSpec((depth, units), lambda k, s: (k, 0))
    out_spec = pl.BlockSpec((rows, units), lambda k, s: (0, 0))
    out = pltpu.HBM((rows, units), jnp.float32)
    return pl.pallas_call(
        functools.partial(project_kernel, block),
        grid_spec=pltpu.PrefetchScalarGridSpec(
            num_scalar_prefetch=1,
            grid=(width // depth,),
            in_specs=[weight_spec, weight_spec, ANY_SPEC, ANY_SPEC],
            out_specs=[out_spec, out_spec],
            scratch_shapes=[
                pltpu.VMEM((rows, width), jnp.bfloat16),
                pltpu.SemaphoreType.DMA((rows // block,)),
            ],
        ),
        out_shape=[out, out],
        compiler_params=pltpu.CompilerParams(vmem_limit_bytes=rows * width * 2 + 20 * MIB),
        cost_estimate=pl.CostEstimate(
            flops=4 * rows * width * units,
            bytes_accessed=2 * (rows + 2 * units) * width,
            transcendentals=rows * units,
        ),
        name="project",
    )(me, *in_hbm([gate_weight, up_weight, own, other]))


def combine_kernel(pick_ref, gate_ref, up_ref, products_ref, out_ref):
    delta = jnp.dot(pick_ref[...], products_ref[...], preferred_element_type=jnp.float32)
    out_ref[...] = (gate_ref[...] * (up_ref[...] + delta)).astype(out_ref.dtype)


def combine(pick, gate, up, products):
    rows, units = gate.shape
    slots_all = products.shape[0]
    tile = min(512, units)
    column_spec = pl.BlockSpec((rows, tile), lambda n: (0, n))
    return pl.pallas_call(
        combine_kernel,
        grid=(units // tile,),
        in_specs=[
            pl.BlockSpec((rows, slots_all), lambda n: (0, 0)),
            column_spec,
            column_spec,
            pl.BlockSpec((slots_all, tile), lambda n: (0, n)),
        ],
        out_specs=column_spec,
        out_shape=pltpu.HBM((rows, units), jnp.bfloat16),
        compiler_params=pltpu.CompilerParams(vmem_limit_bytes=rows * slots_all * 4 + 20 * MIB),
        cost_estimate=pl.CostEstimate(
            flops=2 * rows * slots_all * units, bytes_accessed=10 * rows * units, transcendentals=0
        ),
        name="combine",
    )(*in_hbm([pick, gate, up]), products)


def per_device(
    tokens,
    gate_weight,
    up_weight,
    adapter_down_weight,
    adapter_up_weight,
    row_adapter,
    sorted_rows,
    segment_count,
):
    axis = "tensor"
    size = lax.axis_size(axis)
    me = lax.axis_index(axis).astype(jnp.int32)
    chips = size // CORES
    resident, rank, width = adapter_down_weight.shape
    ranks = resident * rank
    rows = row_adapter.shape[0]
    block = tokens.shape[0]
    me_array = me.reshape(1)
    flips = [(d, d ^ 1) for d in range(size)]

    def other_core(value):
        return lax.ppermute(value, axis, flips)

    most = CORES * resident * ROWS_PER_LIMIT
    sizes = [slots for slots in SLOT_SIZES if slots < most] + [most]
    groups = lax.axis_size("groups")
    own_down = adapter_down_weight.reshape(ranks, width)
    own_maps = adapter_up_weight.reshape(ranks, -1)
    other_down = other_core(own_down)
    counts = [segment_count] + [
        lax.ppermute(segment_count, "groups", [(g, (g + shift) % groups) for g in range(groups)])
        for shift in range(1, groups)
    ]
    other_maps = other_core(own_maps)

    def beside(step, values):
        nonlocal other_down, counts, other_maps
        if step == 1:
            other_down, counts, values[1] = lax.optimization_barrier((other_down, counts, values[1]))
        return values

    pieces = ring_gather(tokens, axis, beside)
    own_tokens, own_shrunk, held, choice = shrink(
        me_array, counts, sorted_rows, pieces, own_down, other_down, sizes
    )
    other_shrunk = other_core(own_shrunk)

    same_core = [[c * CORES + k for c in range(chips)] for k in range(CORES)]

    def finish(slots):
        def branch(own_tokens, own_shrunk, other_shrunk, own_maps, other_maps, held, gate_weight, up_weight):
            products = expand(
                segment_count, me_array, held, own_shrunk, other_shrunk, own_maps, other_maps, slots, block
            )
            products = lax.all_to_all(
                products, axis, split_axis=0, concat_axis=0, axis_index_groups=same_core, tiled=True
            )
            held, other_tokens = lax.optimization_barrier((held, other_core(own_tokens)))
            held_rows = held[:, :slots].reshape(1, chips * slots)
            pick = (jnp.arange(rows, dtype=jnp.int32)[:, None] == held_rows).astype(jnp.bfloat16)
            pick, other_tokens = lax.optimization_barrier((pick, other_tokens))
            gate, up = project(me_array, own_tokens, other_tokens, gate_weight, up_weight, block)
            return combine(pick, gate, up, products.reshape(chips * slots, -1))

        return branch

    return lax.switch(
        choice[0],
        [finish(slots) for slots in sizes],
        own_tokens,
        own_shrunk,
        other_shrunk,
        own_maps,
        other_maps,
        held,
        gate_weight,
        up_weight,
    )


def solution(mesh):
    placed = (
        P(("groups", "tensor"), None),
        P(None, "tensor"),
        P(None, "tensor"),
        P(("groups", "tensor"), None, None),
        P(("groups", "tensor"), None, None),
        P("groups"),
        P("groups"),
        P("groups"),
    )
    return jax.shard_map(
        per_device, mesh=mesh, in_specs=placed, out_specs=P("groups", "tensor"), check_vma=False
    )
```

profile of v0, /device:TPU:0, one launch (start us, length us, event | category | flops | bytes accessed | tf_op | source)
XLA Modules:
  0.0 80.4 jit_solution(16828632112049807470)
XLA Ops:
  0.0 0.5 collective-permute-start.20
  0.5 1.0 %fusion.3 = (bf16[16,4096]{1,0:T(8,128)(2,1)S(1)}, bf16[16,4096]{1,0:T(8,128)(2,1)S(1)}) fusion(bf16[16,8192]{1,0:T(8,128)(2,1)} %refs_5_.1), kind=kLoop, calls=%fused_computation.6 | loop fusion | bytes 524288 | tf_op jit(solution)/shard_map/slice | solution.py:43
  1.5 3.1 %collective-permute-start.7 = (bf16[16,4096]{1,0:T(8,128)(2,1)S(1)}, bf16[16,4096]{1,0:T(8,128)(2,1)S(1)}, u32[]{:S(2)}, u32[]{:S(2)}) collective-permute-start(bf16[16,4096]{1,0:T(8,128)(2,1)S(1)} %get-tuple-element.152), channel_id=1, source_target_pairs={{0,4},{1,5},{4,8},{5,9},{8,12},{9,13},{12,14},{13,15},{14,10},{15,... | collective-permute-start | bytes 393224 | tf_op jit(solution)/shard_map/ppermute | solution.py:39
  4.6 1.5 %collective-permute-start.4 = (s32[16]{0:T(128)}, s32[16]{0:T(128)S(1)}, u32[]{:S(2)}, u32[]{:S(2)}) collective-permute-start(s32[16]{0:T(128)} %refs_0_), channel_id=1, source_target_pairs={{0,16},{16,0},{1,17},{17,1},{2,18},{18,2},{3,19},{19,3},{4,20},{20... | collective-permute-start | bytes 200 | tf_op jit(solution)/shard_map/ppermute | solution.py:414
  6.1 0.4 collective-permute-start.6
  6.5 1.7 %collective-permute-done.4.refs_1_ = s32[16]{0:T(128)S(1)} collective-permute-done((s32[16]{0:T(128)}, s32[16]{0:T(128)S(1)}, u32[]{:S(2)}, u32[]{:S(2)}) %collective-permute-start.4) | collective-permute-done | bytes 96 | tf_op jit(solution)/shard_map/ppermute | solution.py:414
  8.3 2.0 %collective-permute-start.5 = (bf16[16,4096]{1,0:T(8,128)(2,1)S(1)}, bf16[16,4096]{1,0:T(8,128)(2,1)S(1)}, u32[]{:S(2)}, u32[]{:S(2)}) collective-permute-start(bf16[16,4096]{1,0:T(8,128)(2,1)S(1)} %get-tuple-element.153), channel_id=1, source_target_pairs={{0,4},{1,5},{4,8},{5,9},{8,12},{9,13},{12,14},{13,15},{14,10},{15,... | collective-permute-start | bytes 393224 | tf_op jit(solution)/shard_map/ppermute | solution.py:39
  10.3 2.1 %collective-permute-done.6.refs_9_ = bf16[16,4096]{1,0:T(8,128)(2,1)S(1)} collective-permute-done((bf16[16,4096]{1,0:T(8,128)(2,1)S(1)}, bf16[16,4096]{1,0:T(8,128)(2,1)S(1)}, u32[]{:S(2)}, u32[]{:S(2)}) %collective-permute-start.6) | collective-permute-done | bytes 131104 | tf_op jit(solution)/shard_map/ppermute | solution.py:39
  12.4 1.6 %collective-permute-start.9 = (bf16[16,4096]{1,0:T(8,128)(2,1)S(1)}, bf16[16,4096]{1,0:T(8,128)(2,1)S(1)}, u32[]{:S(2)}, u32[]{:S(2)}) collective-permute-start(bf16[16,4096]{1,0:T(8,128)(2,1)S(1)} %collective-permute-done.7.refs_6_), channel_id=1, source_target_pairs={{0,4},{1,5},{4,8},{5,9},{8,12},{9,13},{12,14},{13,15},{14,10},{15,... | collective-permute-start | bytes 393224 | tf_op jit(solution)/shard_map/ppermute | solution.py:39
  13.9 0.4 collective-permute-start.10
  14.6 1.7 %collective-permute-start.11 = (bf16[16,4096]{1,0:T(8,128)(2,1)S(1)}, bf16[16,4096]{1,0:T(8,128)(2,1)S(1)}, u32[]{:S(2)}, u32[]{:S(2)}) collective-permute-start(bf16[16,4096]{1,0:T(8,128)(2,1)S(1)} %collective-permute-done.5.refs_8_), channel_id=1, source_target_pairs={{0,4},{1,5},{4,8},{5,9},{8,12},{9,13},{12,14},{13,15},{14,10},{15,... | collective-permute-start | bytes 393224 | tf_op jit(solution)/shard_map/ppermute | solution.py:39
  16.6 2.1 %collective-permute-done.9.refs_10_ = bf16[16,4096]{1,0:T(8,128)(2,1)S(1)} collective-permute-done((bf16[16,4096]{1,0:T(8,128)(2,1)S(1)}, bf16[16,4096]{1,0:T(8,128)(2,1)S(1)}, u32[]{:S(2)}, u32[]{:S(2)}) %collective-permute-start.9) | collective-permute-done | bytes 131104 | tf_op jit(solution)/shard_map/ppermute | solution.py:39
  18.7 1.6 %collective-permute-start.13 = (bf16[16,4096]{1,0:T(8,128)(2,1)S(1)}, bf16[16,4096]{1,0:T(8,128)(2,1)S(1)}, u32[]{:S(2)}, u32[]{:S(2)}) collective-permute-start(bf16[16,4096]{1,0:T(8,128)(2,1)S(1)} %collective-permute-done.9.refs_10_), channel_id=1, source_target_pairs={{0,4},{1,5},{4,8},{5,9},{8,12},{9,13},{12,14},{13,15},{14,10},{15,... | collective-permute-start | bytes 393224 | tf_op jit(solution)/shard_map/ppermute | solution.py:39
  20.2 0.5 collective-permute-start.14
  20.7 0.8 collective-permute-done.11.refs_12_
  21.5 1.6 %collective-permute-start.15 = (bf16[16,4096]{1,0:T(8,128)(2,1)S(1)}, bf16[16,4096]{1,0:T(8,128)(2,1)S(1)}, u32[]{:S(2)}, u32[]{:S(2)}) collective-permute-start(bf16[16,4096]{1,0:T(8,128)(2,1)S(1)} %collective-permute-done.11.refs_12_), channel_id=1, source_target_pairs={{0,4},{1,5},{4,8},{5,9},{8,12},{9,13},{12,14},{13,15},{14,10},{15,... | collective-permute-start | bytes 393224 | tf_op jit(solution)/shard_map/ppermute | solution.py:39
  23.0 0.5 collective-permute-start.16
  23.5 0.9 %collective-permute-done.13.refs_14_ = bf16[16,4096]{1,0:T(8,128)(2,1)S(1)} collective-permute-done((bf16[16,4096]{1,0:T(8,128)(2,1)S(1)}, bf16[16,4096]{1,0:T(8,128)(2,1)S(1)}, u32[]{:S(2)}, u32[]{:S(2)}) %collective-permute-start.13) | collective-permute-done | bytes 131104 | tf_op jit(solution)/shard_map/ppermute | solution.py:39
  24.4 1.5 %collective-permute-start.17 = (bf16[16,4096]{1,0:T(8,128)(2,1)S(1)}, bf16[16,4096]{1,0:T(8,128)(2,1)S(1)}, u32[]{:S(2)}, u32[]{:S(2)}) collective-permute-start(bf16[16,4096]{1,0:T(8,128)(2,1)S(1)} %collective-permute-done.13.refs_14_), channel_id=1, source_target_pairs={{0,4},{1,5},{4,8},{5,9},{8,12},{9,13},{12,14},{13,15},{14,10},{15,... | collective-permute-start | bytes 393224 | tf_op jit(solution)/shard_map/ppermute | solution.py:39
  25.9 0.5 collective-permute-start.18
  26.5 1.5 %collective-permute-done.16.refs_17_ = bf16[16,4096]{1,0:T(8,128)(2,1)S(1)} collective-permute-done((bf16[16,4096]{1,0:T(8,128)(2,1)S(1)}, bf16[16,4096]{1,0:T(8,128)(2,1)S(1)}, u32[]{:S(2)}, u32[]{:S(2)}) %collective-permute-start.16) | collective-permute-done | bytes 131104 | tf_op jit(solution)/shard_map/ppermute | solution.py:39
  28.0 0.7 copy-done
  28.7 4.4 %shrink_near.1 = (bf16[128,8192]{1,0:T(8,128)(2,1)}, bf16[128,128]{1,0:T(8,128)(2,1)S(1)}, s32[8,128]{1,0:T(8,128)S(1)}, s32[1]{0:T(128)}) custom-call(s32[1]{0:T(128)} %bitcast.4.me, s32[16]{0:T(128)} %refs_0_, s32[16]{0:T(128)S(1)} %collective-permute-done.4.refs_1_, s32[1,256]{1,0:T(1,128)S(1)} %bitcast.14, bf16[64,8192]{1,0:T(8,128)(2,1)} %bitcast.20, ...), custom_call_target="tpu_custom_call" | custom-call | tf_op jit(solution)/shard_map/shrink_near/pallas_call | solution.py:165
  33.1 2.3 %shrink_far.1 = (bf16[128,8192]{1,0:T(8,128)(2,1)}, bf16[128,128]{1,0:T(8,128)(2,1)S(1)}) custom-call(s32[1]{0:T(128)} %bitcast.4.me, bf16[128,8192]{1,0:T(8,128)(2,1)} %get-tuple-element.134.tokens_in, bf16[128,128]{1,0:T(8,128)(2,1)S(1)} %get-tuple-element.135.shrunk_in, bf16[64,8192]{1,0:T(8,128)(2,1)} %bitcast.21, ...), custom_call_target="tpu_custom_call", output_to_operand_aliasing={{0}: (1, {})} | custom-call | tf_op jit(solution)/shard_map/shrink_far/pallas_call | solution.py:187
  36.1 0.5 collective-permute-done.19
  36.7 43.7 %conditional.1 = (bf16[256,1024]{1,0:T(8,128)(2,1)}) conditional(s32[]{:T(128)} %bitcast.7, (bf16[128,8192]{1,0:T(8,128)(2,1)}, s32[8,128]{1,0:T(8,128)S(1)}, s32[1]{0:T(128)}, bf16[8192,1024]{1,0:T(8,128)(2,1)}, bf16[8192,1024]{1,0:T(8,128)(2,1)}, /*index=5*/s32[16]{0:T(128)S(1)}, bf16[128,128]{1,0:T(8,128)(2,1)S(1)}, ...), branch_computations={%region_0.0_spmd, %region_1.0_spmd, %region_2.0_spmd} | conditional | flops 9395765248 | bytes 68161640 | solution.py:450
  36.9 4.0 %expand.3 = bf16[8,80,1024]{2,1,0:T(8,128)(2,1)} custom-call(s32[16]{0:T(128)S(1)} %get-tuple-element.80.counts, s32[1]{0:T(128)} %get-tuple-element.74.me, s32[8,128]{1,0:T(8,128)S(1)} %get-tuple-element.71.held_ref, bf16[128,128]{1,0:T(8,128)(2,1)S(1)} %get-tuple-element.81.own_ref, bf16[128,128]{1,0:T(8,128)(2,1)S(1)} %get-tuple-element.82.other_ref, ...), custom_call_target="tpu_custom_call" | custom-call | flops 167772160 | bytes 3407872 | tf_op jit(solution)/shard_map/cond/branch_0_fun/expand/pallas_call | solution.py:264
  40.9 4.8 %all-to-all-start = ((bf16[8,80,1024]{2,1,0:T(8,128)(2,1)}), bf16[8,80,1024]{2,1,0:T(8,128)(2,1)S(1)}, u32[]{:S(2)}, u32[]{:S(2)}) async-start(bf16[8,80,1024]{2,1,0:T(8,128)(2,1)} %expand.3), calls=%async_computation | async-start | bytes 2621440 | tf_op jit(solution)/shard_map/cond/branch_0_fun/all_to_all | solution.py:438
  45.8 0.9 %fusion.pick_ref = bf16[256,640]{1,0:T(8,128)(2,1)} fusion(s32[640]{0:T(1024)S(1)} %eq.19), kind=kLoop, calls=%fused_computation.1 | loop fusion | flops 327680 | bytes 330240 | tf_op jit(solution)/shard_map/cond/branch_0_fun/convert_element_type | solution.py:443
  47.2 20.2 %project.3 = (f32[256,1024]{1,0:T(8,128)}, f32[256,1024]{1,0:T(8,128)}) custom-call(s32[1]{0:T(128)} %get-tuple-element.74.me, bf16[8192,1024]{1,0:T(8,128)(2,1)} %get-tuple-element.146.gate_weight_ref, bf16[8192,1024]{1,0:T(8,128)(2,1)} %get-tuple-element.149.up_weight_ref, bf16[128,8192]{1,0:T(8,128)(2,1)} %get-tuple-element.70.own_ref, ...), custom_call_target="tpu_custom_call" | custom-call | flops 8589934592 | bytes 37748736 | tf_op jit(solution)/shard_map/cond/branch_0_fun/project/pallas_call | solution.py:331
  67.4 10.2 %all-to-all-done = bf16[8,80,1024]{2,1,0:T(8,128)(2,1)S(1)} async-done(((bf16[8,80,1024]{2,1,0:T(8,128)(2,1)}), bf16[8,80,1024]{2,1,0:T(8,128)(2,1)S(1)}, u32[]{:S(2)}, u32[]{:S(2)}) %all-to-all-start) | async-done | bytes 1310752 | tf_op jit(solution)/shard_map/cond/branch_0_fun/all_to_all | solution.py:438
  77.6 2.8 %combine.3 = bf16[256,1024]{1,0:T(8,128)(2,1)} custom-call(bf16[256,640]{1,0:T(8,128)(2,1)} %fusion.pick_ref, f32[256,1024]{1,0:T(8,128)} %get-tuple-element.78.gate_ref, f32[256,1024]{1,0:T(8,128)} %get-tuple-element.79.up_ref, bf16[640,1024]{1,0:T(8,128)(2,1)S(1)} %bitcast.13), custom_call_target="tpu_custom_call" | custom-call | flops 335544320 | bytes 2621440 | tf_op jit(solution)/shard_map/cond/branch_0_fun/combine/pallas_call | solution.py:364
  (25 shorter events, 1.4 us)
Async XLA Ops:
  0.0 36.7 %collective-permute-start.20 = (bf16[64,16384]{1,0:T(8,128)(2,1)}, bf16[64,16384]{1,0:T(8,128)(2,1)}, u32[]{:S(2)}, u32[]{:S(2)}) collective-permute-start(bf16[64,16384]{1,0:T(8,128)(2,1)} %bitcast.15), channel_id=1, source_target_pairs={{0,1},{1,0},{2,3},{3,2},{4,5},{5,4},{6,7},{7,6},{8,9},{9,8},{10,11... | collective-permute-start | bytes 6291464 | tf_op jit(solution)/shard_map/ppermute | solution.py:405
  0.5 14.1 %collective-permute-start.3 = (bf16[64,8192]{1,0:T(8,128)(2,1)}, bf16[64,8192]{1,0:T(8,128)(2,1)S(1)}, u32[]{:S(2)}, u32[]{:S(2)}) collective-permute-start(bf16[64,8192]{1,0:T(8,128)(2,1)} %bitcast.19), channel_id=1, source_target_pairs={{0,1},{1,0},{2,3},{3,2},{4,5},{5,4},{6,7},{7,6},{8,9},{9,8},{10,11... | collective-permute-start | bytes 3145736 | tf_op jit(solution)/shard_map/ppermute | solution.py:405
  1.5 6.8 %collective-permute-start.7 = (bf16[16,4096]{1,0:T(8,128)(2,1)S(1)}, bf16[16,4096]{1,0:T(8,128)(2,1)S(1)}, u32[]{:S(2)}, u32[]{:S(2)}) collective-permute-start(bf16[16,4096]{1,0:T(8,128)(2,1)S(1)} %get-tuple-element.152), channel_id=1, source_target_pairs={{0,4},{1,5},{4,8},{5,9},{8,12},{9,13},{12,14},{13,15},{14,10},{15,... | collective-permute-start | bytes 393224 | tf_op jit(solution)/shard_map/ppermute | solution.py:39
  4.6 3.7 %collective-permute-start.4 = (s32[16]{0:T(128)}, s32[16]{0:T(128)S(1)}, u32[]{:S(2)}, u32[]{:S(2)}) collective-permute-start(s32[16]{0:T(128)} %refs_0_), channel_id=1, source_target_pairs={{0,16},{16,0},{1,17},{17,1},{2,18},{18,2},{3,19},{19,3},{4,20},{20... | collective-permute-start | bytes 200 | tf_op jit(solution)/shard_map/ppermute | solution.py:414
  6.1 6.3 %collective-permute-start.6 = (bf16[16,4096]{1,0:T(8,128)(2,1)S(1)}, bf16[16,4096]{1,0:T(8,128)(2,1)S(1)}, u32[]{:S(2)}, u32[]{:S(2)}) collective-permute-start(bf16[16,4096]{1,0:T(8,128)(2,1)S(1)} %get-tuple-element.152), channel_id=1, source_target_pairs={{0,2},{1,3},{4,0},{5,1},{8,4},{9,5},{12,8},{13,9},{14,12},{15,13},... | collective-permute-start | bytes 393224 | tf_op jit(solution)/shard_map/ppermute | solution.py:39
  8.3 5.7 %collective-permute-start.8 = (bf16[16,4096]{1,0:T(8,128)(2,1)S(1)}, bf16[16,4096]{1,0:T(8,128)(2,1)S(1)}, u32[]{:S(2)}, u32[]{:S(2)}) collective-permute-start(bf16[16,4096]{1,0:T(8,128)(2,1)S(1)} %get-tuple-element.153), channel_id=1, source_target_pairs={{0,2},{1,3},{4,0},{5,1},{8,4},{9,5},{12,8},{13,9},{14,12},{15,13},... | collective-permute-start | bytes 393224 | tf_op jit(solution)/shard_map/ppermute | solution.py:39
  8.3 6.3 %collective-permute-start.5 = (bf16[16,4096]{1,0:T(8,128)(2,1)S(1)}, bf16[16,4096]{1,0:T(8,128)(2,1)S(1)}, u32[]{:S(2)}, u32[]{:S(2)}) collective-permute-start(bf16[16,4096]{1,0:T(8,128)(2,1)S(1)} %get-tuple-element.153), channel_id=1, source_target_pairs={{0,4},{1,5},{4,8},{5,9},{8,12},{9,13},{12,14},{13,15},{14,10},{15,... | collective-permute-start | bytes 393224 | tf_op jit(solution)/shard_map/ppermute | solution.py:39
  12.4 6.3 %collective-permute-start.9 = (bf16[16,4096]{1,0:T(8,128)(2,1)S(1)}, bf16[16,4096]{1,0:T(8,128)(2,1)S(1)}, u32[]{:S(2)}, u32[]{:S(2)}) collective-permute-start(bf16[16,4096]{1,0:T(8,128)(2,1)S(1)} %collective-permute-done.7.refs_6_), channel_id=1, source_target_pairs={{0,4},{1,5},{4,8},{5,9},{8,12},{9,13},{12,14},{13,15},{14,10},{15,... | collective-permute-start | bytes 393224 | tf_op jit(solution)/shard_map/ppermute | solution.py:39
  13.9 6.3 %collective-permute-start.10 = (bf16[16,4096]{1,0:T(8,128)(2,1)S(1)}, bf16[16,4096]{1,0:T(8,128)(2,1)S(1)}, u32[]{:S(2)}, u32[]{:S(2)}) collective-permute-start(bf16[16,4096]{1,0:T(8,128)(2,1)S(1)} %collective-permute-done.8.refs_7_), channel_id=1, source_target_pairs={{0,2},{1,3},{4,0},{5,1},{8,4},{9,5},{12,8},{13,9},{14,12},{15,13},... | collective-permute-start | bytes 393224 | tf_op jit(solution)/shard_map/ppermute | solution.py:39
  14.6 13.4 %copy-start.1 = (bf16[64,8192]{1,0:T(8,128)(2,1)}, bf16[64,8192]{1,0:T(8,128)(2,1)S(1)}, u32[]{:S(2)}) copy-start(bf16[64,8192]{1,0:T(8,128)(2,1)S(1)} %collective-permute-done.3.refs_4_.other_down_ref) | copy-start | bytes 3145732
  14.6 6.9 %collective-permute-start.11 = (bf16[16,4096]{1,0:T(8,128)(2,1)S(1)}, bf16[16,4096]{1,0:T(8,128)(2,1)S(1)}, u32[]{:S(2)}, u32[]{:S(2)}) collective-permute-start(bf16[16,4096]{1,0:T(8,128)(2,1)S(1)} %collective-permute-done.5.refs_8_), channel_id=1, source_target_pairs={{0,4},{1,5},{4,8},{5,9},{8,12},{9,13},{12,14},{13,15},{14,10},{15,... | collective-permute-start | bytes 393224 | tf_op jit(solution)/shard_map/ppermute | solution.py:39
  16.3 6.7 %collective-permute-start.12 = (bf16[16,4096]{1,0:T(8,128)(2,1)S(1)}, bf16[16,4096]{1,0:T(8,128)(2,1)S(1)}, u32[]{:S(2)}, u32[]{:S(2)}) collective-permute-start(bf16[16,4096]{1,0:T(8,128)(2,1)S(1)} %collective-permute-done.6.refs_9_), channel_id=1, source_target_pairs={{0,2},{1,3},{4,0},{5,1},{8,4},{9,5},{12,8},{13,9},{14,12},{15,13},... | collective-permute-start | bytes 393224 | tf_op jit(solution)/shard_map/ppermute | solution.py:39
  18.7 5.7 %collective-permute-start.13 = (bf16[16,4096]{1,0:T(8,128)(2,1)S(1)}, bf16[16,4096]{1,0:T(8,128)(2,1)S(1)}, u32[]{:S(2)}, u32[]{:S(2)}) collective-permute-start(bf16[16,4096]{1,0:T(8,128)(2,1)S(1)} %collective-permute-done.9.refs_10_), channel_id=1, source_target_pairs={{0,4},{1,5},{4,8},{5,9},{8,12},{9,13},{12,14},{13,15},{14,10},{15,... | collective-permute-start | bytes 393224 | tf_op jit(solution)/shard_map/ppermute | solution.py:39
  20.2 5.7 %collective-permute-start.14 = (bf16[16,4096]{1,0:T(8,128)(2,1)S(1)}, bf16[16,4096]{1,0:T(8,128)(2,1)S(1)}, u32[]{:S(2)}, u32[]{:S(2)}) collective-permute-start(bf16[16,4096]{1,0:T(8,128)(2,1)S(1)} %collective-permute-done.10.refs_11_), channel_id=1, source_target_pairs={{0,2},{1,3},{4,0},{5,1},{8,4},{9,5},{12,8},{13,9},{14,12},{15,13},... | collective-permute-start | bytes 393224 | tf_op jit(solution)/shard_map/ppermute | solution.py:39
  21.5 5.1 %collective-permute-start.15 = (bf16[16,4096]{1,0:T(8,128)(2,1)S(1)}, bf16[16,4096]{1,0:T(8,128)(2,1)S(1)}, u32[]{:S(2)}, u32[]{:S(2)}) collective-permute-start(bf16[16,4096]{1,0:T(8,128)(2,1)S(1)} %collective-permute-done.11.refs_12_), channel_id=1, source_target_pairs={{0,4},{1,5},{4,8},{5,9},{8,12},{9,13},{12,14},{13,15},{14,10},{15,... | collective-permute-start | bytes 393224 | tf_op jit(solution)/shard_map/ppermute | solution.py:39
  23.0 5.0 %collective-permute-start.16 = (bf16[16,4096]{1,0:T(8,128)(2,1)S(1)}, bf16[16,4096]{1,0:T(8,128)(2,1)S(1)}, u32[]{:S(2)}, u32[]{:S(2)}) collective-permute-start(bf16[16,4096]{1,0:T(8,128)(2,1)S(1)} %collective-permute-done.12.refs_13_), channel_id=1, source_target_pairs={{0,2},{1,3},{4,0},{5,1},{8,4},{9,5},{12,8},{13,9},{14,12},{15,13},... | collective-permute-start | bytes 393224 | tf_op jit(solution)/shard_map/ppermute | solution.py:39
  24.4 8.6 %collective-permute-start.17 = (bf16[16,4096]{1,0:T(8,128)(2,1)S(1)}, bf16[16,4096]{1,0:T(8,128)(2,1)S(1)}, u32[]{:S(2)}, u32[]{:S(2)}) collective-permute-start(bf16[16,4096]{1,0:T(8,128)(2,1)S(1)} %collective-permute-done.13.refs_14_), channel_id=1, source_target_pairs={{0,4},{1,5},{4,8},{5,9},{8,12},{9,13},{12,14},{13,15},{14,10},{15,... | collective-permute-start | bytes 393224 | tf_op jit(solution)/shard_map/ppermute | solution.py:39
  25.9 7.1 %collective-permute-start.18 = (bf16[16,4096]{1,0:T(8,128)(2,1)S(1)}, bf16[16,4096]{1,0:T(8,128)(2,1)S(1)}, u32[]{:S(2)}, u32[]{:S(2)}) collective-permute-start(bf16[16,4096]{1,0:T(8,128)(2,1)S(1)} %collective-permute-done.14.refs_15_), channel_id=1, source_target_pairs={{0,2},{1,3},{4,0},{5,1},{8,4},{9,5},{12,8},{13,9},{14,12},{15,13},... | collective-permute-start | bytes 393224 | tf_op jit(solution)/shard_map/ppermute | solution.py:39
  28.0 0.7 copy-start
  33.1 3.6 %copy-start.4 = (s32[16]{0:T(128)S(1)}, s32[16]{0:T(128)}, u32[]{:S(2)}) copy-start(s32[16]{0:T(128)} %refs_0_) | copy-start | bytes 196
  35.4 1.3 %collective-permute-start.19 = (bf16[128,128]{1,0:T(8,128)(2,1)S(1)}, bf16[128,128]{1,0:T(8,128)(2,1)S(1)}, u32[]{:S(2)}, u32[]{:S(2)}) collective-permute-start(bf16[128,128]{1,0:T(8,128)(2,1)S(1)} %get-tuple-element.138), channel_id=1, source_target_pairs={{0,1},{1,0},{2,3},{3,2},{4,5},{5,4},{6,7},{7,6},{8,9},{9,8},{10,11... | collective-permute-start | bytes 98312 | tf_op jit(solution)/shard_map/ppermute | solution.py:405
  36.7 9.0 %collective-permute-start = (bf16[128,8192]{1,0:T(8,128)(2,1)}, bf16[128,8192]{1,0:T(8,128)(2,1)S(1)}, u32[]{:S(2)}, u32[]{:S(2)}) collective-permute-start(bf16[128,8192]{1,0:T(8,128)(2,1)} %get-tuple-element.70.own_ref), channel_id=1, source_target_pairs={{0,1},{1,0},{2,3},{3,2},{4,5},{5,4},{6,7},{7,6},{8,9},{9,8},{10,11... | collective-permute-start | bytes 6291464 | tf_op jit(solution)/shard_map/cond/branch_0_fun/ppermute | solution.py:405
  40.9 36.7 %all-to-all-start = ((bf16[8,80,1024]{2,1,0:T(8,128)(2,1)}), bf16[8,80,1024]{2,1,0:T(8,128)(2,1)S(1)}, u32[]{:S(2)}, u32[]{:S(2)}) async-start(bf16[8,80,1024]{2,1,0:T(8,128)(2,1)} %expand.3), calls=%async_computation | async-start | bytes 2621440 | tf_op jit(solution)/shard_map/cond/branch_0_fun/all_to_all | solution.py:438
  45.7 1.4 %copy-start.2 = (bf16[128,8192]{1,0:T(8,128)(2,1)}, bf16[128,8192]{1,0:T(8,128)(2,1)S(1)}, u32[]{:S(2)}) copy-start(bf16[128,8192]{1,0:T(8,128)(2,1)S(1)} %collective-permute-done.other_ref) | copy-start | bytes 6291460 | tf_op jit(solution)/shard_map/cond
where the time goes:
time: 80.7 us; the launch traced here: 80.4 us
  Pallas kernels  33.7 us (42%)
  starting transfers between devices  22.7 us (28%)
  waiting for transfers between devices  20.1 us (25%)
  local copies, waits for them, and re-layouts  2.17 us (3%)
  other arithmetic  0.94 us (1%)
    pallas_call x1, Pallas kernels, project(): pl.pallas_call(functools.partial(project_kernel, block), grid_spec=pltpu....  20.2 us
    ppermute x14, starting transfers between devices, moved(): return lax.ppermute(value, axis, pairs)  15.7 us
    all_to_all x1, waiting for transfers between devices, branch(): lax.all_to_all(products, axis, split_axis=0, concat_axis=0, axis_index_gr...  10.2 us
    ppermute x14, waiting for transfers between devices, moved(): return lax.ppermute(value, axis, pairs)  7.59 us
    all_to_all x1, starting transfers between devices, branch(): lax.all_to_all(products, axis, split_axis=0, concat_axis=0, axis_index_gr...  4.82 us
    pallas_call x1, Pallas kernels, shrink(): pl.pallas_call(functools.partial(shrink_near_kernel, sizes, [place[1:] fo...  4.35 us
    pallas_call x1, Pallas kernels, expand(): pl.pallas_call(functools.partial(expand_kernel, block), grid_spec=pltpu.P...  4.04 us
    pallas_call x1, Pallas kernels, combine(): pl.pallas_call(combine_kernel, grid=(units // tile,), in_specs=[pl.BlockS...  2.78 us
  transfers between devices with their start and end apart: 20, of which 10 were waited for; matrix products, arithmetic and copies ran while one was open for 2% of the time, Pallas kernels for 38%

commit v1 on v0

--- a/solution.py
+++ b/solution.py
@@ -126,24 +126,38 @@
     out_copy.wait()
 
 
-def shrink_far_kernel(me, tokens_in, shrunk_in, own_down_ref, other_down_ref, *refs):
-    piece_refs = refs[:2]
-    tokens_ref, shrunk_ref, far_vmem, down_vmem, sems = refs[2:]
-    rows, width = far_vmem.shape
+def shrink_far_kernel(places, me, tokens_in, shrunk_in, own_down_ref, other_down_ref, *refs):
+    piece_refs = refs[: len(places)]
+    tokens_ref, shrunk_ref, far_vmem, down_vmem, sems = refs[len(places) :]
+    rows, half = piece_refs[0].shape
     chips = tokens_in.shape[0] // rows
-    start = pl.multiple_of(ring_chip(me[0], chips, chips // 2) * rows, rows)
+    slots = {distance % chips: i for i, distance in enumerate(range(chips // 2 - 1, chips // 2 + 2))}
     copies = down_copies(me[0] % CORES, own_down_ref, other_down_ref, down_vmem, sems)
-    half = width // 2
-    for i, ref in enumerate(piece_refs):
-        copies.append(pltpu.make_async_copy(ref, far_vmem.at[:, pl.ds(i * half, half)], sems.at[2 + i]))
+    for ref, (column, distance) in zip(piece_refs, places):
+        slot = slots[distance % chips]
+        copies.append(
+            pltpu.make_async_copy(
+                ref, far_vmem.at[pl.ds(slot * rows, rows), pl.ds(column, half)], sems.at[len(copies)]
+            )
+        )
     run_copies(copies)
-    out_copy = pltpu.make_async_copy(far_vmem, tokens_ref.at[pl.ds(start, rows)], sems.at[4])
-    out_copy.start()
-    shrunk_ref[...] = shrunk_in[...]
-    shrunk_ref[pl.ds(start, rows), :] = lax.dot_general(
+    starts = [pl.multiple_of(ring_chip(me[0], chips, distance) * rows, rows) for distance in slots]
+    out_copies = [
+        pltpu.make_async_copy(
+            far_vmem.at[pl.ds(i * rows, rows)], tokens_ref.at[pl.ds(start, rows)], sems.at[len(copies) + i]
+        )
+        for i, start in enumerate(starts)
+    ]
+    for copy in out_copies:
+        copy.start()
+    shrunk = lax.dot_general(
         far_vmem[...], down_vmem[...], (((1,), (1,)), ((), ())), preferred_element_type=jnp.float32
     ).astype(shrunk_ref.dtype)
-    out_copy.wait()
+    shrunk_ref[...] = shrunk_in[...]
+    for i, start in enumerate(starts):
+        shrunk_ref[pl.ds(start, rows), :] = shrunk[i * rows : (i + 1) * rows]
+    for copy in out_copies:
+        copy.wait()
 
 
 def shrink(me, counts, sorted_rows, pieces, own_down, other_down, sizes):
@@ -151,7 +165,7 @@
     rows_all = sorted_rows.shape[0]
     rows = rows_all // CORES
     values = [value for value, _, _ in pieces]
-    near = values[:-2]
+    near = values[:-6]
     block = values[0].shape[0]
     tokens_shape = pltpu.HBM((rows, width), jnp.bfloat16)
     shrunk_shape = jax.ShapeDtypeStruct((rows, CORES * ranks), jnp.bfloat16)
@@ -163,7 +177,7 @@
     down_vmem = pltpu.VMEM((CORES * ranks, width), jnp.bfloat16)
     downs = in_hbm([own_down, other_down])
     tokens, shrunk, held, choice = pl.pallas_call(
-        functools.partial(shrink_near_kernel, sizes, [place[1:] for place in pieces[:-2]], len(counts)),
+        functools.partial(shrink_near_kernel, sizes, [place[1:] for place in pieces[:-6]], len(counts)),
         grid_spec=pltpu.PrefetchScalarGridSpec(
             num_scalar_prefetch=1 + len(counts),
             grid=(1,),
@@ -183,25 +197,25 @@
         out_shape=[tokens_shape, shrunk_shape, held_shape, jax.ShapeDtypeStruct((1,), jnp.int32)],
         compiler_params=pltpu.CompilerParams(vmem_limit_bytes=rows * width * 2 + 16 * MIB),
         name="shrink_near",
-    )(me, *counts, sorted_rows.reshape(1, rows_all), *downs, *in_hbm(near[:1]), *near[1:])
+    )(me, *counts, *in_hbm([sorted_rows.reshape(1, rows_all)]), *downs, *in_hbm(near[:1]), *near[1:])
     tokens, shrunk = pl.pallas_call(
-        shrink_far_kernel,
+        functools.partial(shrink_far_kernel, [place[1:] for place in pieces[-6:]]),
         grid_spec=pltpu.PrefetchScalarGridSpec(
             num_scalar_prefetch=1,
             grid=(1,),
-            in_specs=[ANY_SPEC, whole(shrunk_shape.shape)] + [ANY_SPEC] * 4,
+            in_specs=[ANY_SPEC, whole(shrunk_shape.shape)] + [ANY_SPEC] * 8,
             out_specs=[ANY_SPEC, whole(shrunk_shape.shape)],
             scratch_shapes=[
-                pltpu.VMEM((block, width), jnp.bfloat16),
+                pltpu.VMEM((3 * block, width), jnp.bfloat16),
                 down_vmem,
-                pltpu.SemaphoreType.DMA((5,)),
+                pltpu.SemaphoreType.DMA((11,)),
             ],
         ),
         out_shape=[tokens_shape, shrunk_shape],
         input_output_aliases={1: 0},
         compiler_params=pltpu.CompilerParams(vmem_limit_bytes=16 * MIB),
         name="shrink_far",
-    )(me, *in_hbm([tokens]), shrunk, *downs, *values[-2:])
+    )(me, *in_hbm([tokens]), shrunk, *downs, *values[-6:])
     return tokens, shrunk, held, choice
 
 

time: 80.7 us -> 81.6 us (1.011)
  Pallas kernels: 33.7 us -> 35.2 us
  starting transfers between devices: 22.7 us -> 23.9 us
  waiting for transfers between devices: 20.1 us -> 19 us
    ppermute x1, waiting for transfers between devices: 1.73 us -> 0.01 us  [per_device(): lax.ppermute(segment_count, 'groups', [(g, (g + shift) % groups) for g in...]
    ppermute x1, starting transfers between devices: 1.49 us -> 2.49 us  [per_device(): lax.ppermute(segment_count, 'groups', [(g, (g + shift) % groups) for g in...]
    pallas_call x1, Pallas kernels: 2.32 us -> 3.21 us  [shrink(): pl.pallas_call(functools.partial(shrink_far_kernel, [place[1:] for place...]
  transfers between devices with their start and end apart: 20 -> 20, of which waited for: 10 -> 8; matrix products, arithmetic and copies ran while one was open for 2% -> 2% of each run, Pallas kernels for 38% -> 40%
where the time goes in v1:
time: 81.6 us; the launch traced here: 81.3 us
  Pallas kernels  35.2 us (43%)
  starting transfers between devices  23.9 us (29%)
  waiting for transfers between devices  19 us (23%)
  local copies, waits for them, and re-layouts  1.51 us (2%)
  other arithmetic  0.93 us (1%)
    pallas_call x1, Pallas kernels, project(): pl.pallas_call(functools.partial(project_kernel, block), grid_spec=pltpu....  20.2 us
    ppermute x14, starting transfers between devices, moved(): return lax.ppermute(value, axis, pairs)  15.3 us
    all_to_all x1, waiting for transfers between devices, branch(): lax.all_to_all(products, axis, split_axis=0, concat_axis=0, axis_index_gr...  10.2 us
    ppermute x14, waiting for transfers between devices, moved(): return lax.ppermute(value, axis, pairs)  8.22 us
    all_to_all x1, starting transfers between devices, branch(): lax.all_to_all(products, axis, split_axis=0, concat_axis=0, axis_index_gr...  5.17 us
    pallas_call x1, Pallas kernels, shrink(): pl.pallas_call(functools.partial(shrink_near_kernel, sizes, [place[1:] fo...  4.96 us
    pallas_call x1, Pallas kernels, expand(): pl.pallas_call(functools.partial(expand_kernel, block), grid_spec=pltpu.P...  4.03 us
    pallas_call x1, Pallas kernels, shrink(): pl.pallas_call(functools.partial(shrink_far_kernel, [place[1:] for place...  3.21 us
  transfers between devices with their start and end apart: 20, of which 8 were waited for; matrix products, arithmetic and copies ran while one was open for 2% of the time, Pallas kernels for 40%

profile of v1, /device:TPU:0, one launch (start us, length us, event | category | flops | bytes accessed | tf_op | source)
XLA Modules:
  0.0 81.3 jit_solution(14317277074397997486)
XLA Ops:
  0.0 0.5 collective-permute-start.20
  0.5 2.5 %collective-permute-start.4 = (s32[16]{0:T(128)}, s32[16]{0:T(128)S(1)}, u32[]{:S(2)}, u32[]{:S(2)}) collective-permute-start(s32[16]{0:T(128)} %refs_0_), channel_id=1, source_target_pairs={{0,16},{16,0},{1,17},{17,1},{2,18},{18,2},{3,19},{19,3},{4,20},{20... | collective-permute-start | bytes 200 | tf_op jit(solution)/shard_map/ppermute | solution.py:428
  3.2 1.0 %fusion.3 = (bf16[16,4096]{1,0:T(8,128)(2,1)S(1)}, bf16[16,4096]{1,0:T(8,128)(2,1)S(1)}) fusion(bf16[16,8192]{1,0:T(8,128)(2,1)} %refs_5_.1), kind=kLoop, calls=%fused_computation.6 | loop fusion | bytes 524288 | tf_op jit(solution)/shard_map/slice | solution.py:43
  4.2 1.6 %collective-permute-start.7 = (bf16[16,4096]{1,0:T(8,128)(2,1)S(1)}, bf16[16,4096]{1,0:T(8,128)(2,1)S(1)}, u32[]{:S(2)}, u32[]{:S(2)}) collective-permute-start(bf16[16,4096]{1,0:T(8,128)(2,1)S(1)} %get-tuple-element.152), channel_id=1, source_target_pairs={{0,4},{1,5},{4,8},{5,9},{8,12},{9,13},{12,14},{13,15},{14,10},{15,... | collective-permute-start | bytes 393224 | tf_op jit(solution)/shard_map/ppermute | solution.py:39
  5.8 0.4 collective-permute-start.8
  6.2 1.5 %collective-permute-start.6 = (bf16[16,4096]{1,0:T(8,128)(2,1)S(1)}, bf16[16,4096]{1,0:T(8,128)(2,1)S(1)}, u32[]{:S(2)}, u32[]{:S(2)}) collective-permute-start(bf16[16,4096]{1,0:T(8,128)(2,1)S(1)} %get-tuple-element.152), channel_id=1, source_target_pairs={{0,2},{1,3},{4,0},{5,1},{8,4},{9,5},{12,8},{13,9},{14,12},{15,13},... | collective-permute-start | bytes 393224 | tf_op jit(solution)/shard_map/ppermute | solution.py:39
  7.8 2.1 %collective-permute-done.7.refs_6_ = bf16[16,4096]{1,0:T(8,128)(2,1)S(1)} collective-permute-done((bf16[16,4096]{1,0:T(8,128)(2,1)S(1)}, bf16[16,4096]{1,0:T(8,128)(2,1)S(1)}, u32[]{:S(2)}, u32[]{:S(2)}) %collective-permute-start.7) | collective-permute-done | bytes 131104 | tf_op jit(solution)/shard_map/ppermute | solution.py:39
  9.9 1.6 %collective-permute-start.9 = (bf16[16,4096]{1,0:T(8,128)(2,1)S(1)}, bf16[16,4096]{1,0:T(8,128)(2,1)S(1)}, u32[]{:S(2)}, u32[]{:S(2)}) collective-permute-start(bf16[16,4096]{1,0:T(8,128)(2,1)S(1)} %collective-permute-done.7.refs_6_), channel_id=1, source_target_pairs={{0,4},{1,5},{4,8},{5,9},{8,12},{9,13},{12,14},{13,15},{14,10},{15,... | collective-permute-start | bytes 393224 | tf_op jit(solution)/shard_map/ppermute | solution.py:39
  11.5 0.7 collective-permute-done.8.refs_7_
  12.2 0.4 collective-permute-start.10
  12.6 2.1 %collective-permute-done.6.refs_9_ = bf16[16,4096]{1,0:T(8,128)(2,1)S(1)} collective-permute-done((bf16[16,4096]{1,0:T(8,128)(2,1)S(1)}, bf16[16,4096]{1,0:T(8,128)(2,1)S(1)}, u32[]{:S(2)}, u32[]{:S(2)}) %collective-permute-start.6) | collective-permute-done | bytes 131104 | tf_op jit(solution)/shard_map/ppermute | solution.py:39
  14.7 1.6 %collective-permute-start.5 = (bf16[16,4096]{1,0:T(8,128)(2,1)S(1)}, bf16[16,4096]{1,0:T(8,128)(2,1)S(1)}, u32[]{:S(2)}, u32[]{:S(2)}) collective-permute-start(bf16[16,4096]{1,0:T(8,128)(2,1)S(1)} %get-tuple-element.153), channel_id=1, source_target_pairs={{0,4},{1,5},{4,8},{5,9},{8,12},{9,13},{12,14},{13,15},{14,10},{15,... | collective-permute-start | bytes 393224 | tf_op jit(solution)/shard_map/ppermute | solution.py:39
  16.3 1.6 %collective-permute-start.13 = (bf16[16,4096]{1,0:T(8,128)(2,1)S(1)}, bf16[16,4096]{1,0:T(8,128)(2,1)S(1)}, u32[]{:S(2)}, u32[]{:S(2)}) collective-permute-start(bf16[16,4096]{1,0:T(8,128)(2,1)S(1)} %collective-permute-done.9.refs_10_), channel_id=1, source_target_pairs={{0,4},{1,5},{4,8},{5,9},{8,12},{9,13},{12,14},{13,15},{14,10},{15,... | collective-permute-start | bytes 393224 | tf_op jit(solution)/shard_map/ppermute | solution.py:39
  17.8 0.5 collective-permute-start.14
  18.3 1.7 %collective-permute-done.5.refs_8_ = bf16[16,4096]{1,0:T(8,128)(2,1)S(1)} collective-permute-done((bf16[16,4096]{1,0:T(8,128)(2,1)S(1)}, bf16[16,4096]{1,0:T(8,128)(2,1)S(1)}, u32[]{:S(2)}, u32[]{:S(2)}) %collective-permute-start.5) | collective-permute-done | bytes 131104 | tf_op jit(solution)/shard_map/ppermute | solution.py:39
  20.0 1.6 %collective-permute-start.11 = (bf16[16,4096]{1,0:T(8,128)(2,1)S(1)}, bf16[16,4096]{1,0:T(8,128)(2,1)S(1)}, u32[]{:S(2)}, u32[]{:S(2)}) collective-permute-start(bf16[16,4096]{1,0:T(8,128)(2,1)S(1)} %collective-permute-done.5.refs_8_), channel_id=1, source_target_pairs={{0,4},{1,5},{4,8},{5,9},{8,12},{9,13},{12,14},{13,15},{14,10},{15,... | collective-permute-start | bytes 393224 | tf_op jit(solution)/shard_map/ppermute | solution.py:39
  22.0 0.8 collective-permute-done.13.refs_0_
  22.8 1.6 %collective-permute-start.17 = (bf16[16,4096]{1,0:T(8,128)(2,1)S(1)}, bf16[16,4096]{1,0:T(8,128)(2,1)S(1)}, u32[]{:S(2)}, u32[]{:S(2)}) collective-permute-start(bf16[16,4096]{1,0:T(8,128)(2,1)S(1)} %collective-permute-done.13.refs_0_), channel_id=1, source_target_pairs={{0,4},{1,5},{4,8},{5,9},{8,12},{9,13},{12,14},{13,15},{14,10},{15,... | collective-permute-start | bytes 393224 | tf_op jit(solution)/shard_map/ppermute | solution.py:39
  24.4 0.4 collective-permute-start.18
  24.9 0.8 %collective-permute-done.11.refs_12_ = bf16[16,4096]{1,0:T(8,128)(2,1)S(1)} collective-permute-done((bf16[16,4096]{1,0:T(8,128)(2,1)S(1)}, bf16[16,4096]{1,0:T(8,128)(2,1)S(1)}, u32[]{:S(2)}, u32[]{:S(2)}) %collective-permute-start.11) | collective-permute-done | bytes 131104 | tf_op jit(solution)/shard_map/ppermute | solution.py:39
  25.7 1.6 %collective-permute-start.15 = (bf16[16,4096]{1,0:T(8,128)(2,1)S(1)}, bf16[16,4096]{1,0:T(8,128)(2,1)S(1)}, u32[]{:S(2)}, u32[]{:S(2)}) collective-permute-start(bf16[16,4096]{1,0:T(8,128)(2,1)S(1)} %collective-permute-done.11.refs_12_), channel_id=1, source_target_pairs={{0,4},{1,5},{4,8},{5,9},{8,12},{9,13},{12,14},{13,15},{14,10},{15,... | collective-permute-start | bytes 393224 | tf_op jit(solution)/shard_map/ppermute | solution.py:39
  27.3 0.4 collective-permute-start.16
  27.7 5.0 %shrink_near.1 = (bf16[128,8192]{1,0:T(8,128)(2,1)}, bf16[128,128]{1,0:T(8,128)(2,1)S(1)}, s32[8,128]{1,0:T(8,128)S(1)}, s32[1]{0:T(128)}) custom-call(s32[1]{0:T(128)} %bitcast.4.me, s32[16]{0:T(128)} %refs_0_, s32[16]{0:T(128)S(1)} %collective-permute-done.4.refs_1_, s32[1,256]{1,0:T(1,128)} %bitcast.24, bf16[64,8192]{1,0:T(8,128)(2,1)} %bitcast.19, ...), custom_call_target="tpu_custom_call" | custom-call | tf_op jit(solution)/shard_map/shrink_near/pallas_call | solution.py:179
  32.7 3.2 %shrink_far.1 = (bf16[128,8192]{1,0:T(8,128)(2,1)}, bf16[128,128]{1,0:T(8,128)(2,1)S(1)}) custom-call(s32[1]{0:T(128)} %bitcast.4.me, bf16[128,8192]{1,0:T(8,128)(2,1)} %get-tuple-element.134.tokens_in, bf16[128,128]{1,0:T(8,128)(2,1)S(1)} %get-tuple-element.135.shrunk_in, bf16[64,8192]{1,0:T(8,128)(2,1)} %bitcast.20, ...), custom_call_target="tpu_custom_call", output_to_operand_aliasing={{0}: (1, {})} | custom-call | tf_op jit(solution)/shard_map/shrink_far/pallas_call | solution.py:201
  36.7 0.5 collective-permute-done.19
  37.2 44.0 %conditional.1 = (bf16[256,1024]{1,0:T(8,128)(2,1)}) conditional(s32[]{:T(128)} %bitcast.7, (bf16[128,8192]{1,0:T(8,128)(2,1)}, s32[8,128]{1,0:T(8,128)S(1)}, s32[1]{0:T(128)}, bf16[8192,1024]{1,0:T(8,128)(2,1)}, bf16[8192,1024]{1,0:T(8,128)(2,1)}, /*index=5*/s32[16]{0:T(128)S(1)}, bf16[128,128]{1,0:T(8,128)(2,1)S(1)}, ...), branch_computations={%region_0.0_spmd, %region_1.0_spmd, %region_2.0_spmd} | conditional | flops 9395765248 | bytes 68161640 | solution.py:464
  37.4 4.0 %expand.3 = bf16[8,80,1024]{2,1,0:T(8,128)(2,1)} custom-call(s32[16]{0:T(128)S(1)} %get-tuple-element.80.counts, s32[1]{0:T(128)} %get-tuple-element.74.me, s32[8,128]{1,0:T(8,128)S(1)} %get-tuple-element.71.held_ref, bf16[128,128]{1,0:T(8,128)(2,1)S(1)} %get-tuple-element.81.own_ref, bf16[128,128]{1,0:T(8,128)(2,1)S(1)} %get-tuple-element.82.other_ref, ...), custom_call_target="tpu_custom_call" | custom-call | flops 167772160 | bytes 3407872 | tf_op jit(solution)/shard_map/cond/branch_0_fun/expand/pallas_call | solution.py:278
  41.4 5.2 %all-to-all-start = ((bf16[8,80,1024]{2,1,0:T(8,128)(2,1)}), bf16[8,80,1024]{2,1,0:T(8,128)(2,1)S(1)}, u32[]{:S(2)}, u32[]{:S(2)}) async-start(bf16[8,80,1024]{2,1,0:T(8,128)(2,1)} %expand.3), calls=%async_computation | async-start | bytes 2621440 | tf_op jit(solution)/shard_map/cond/branch_0_fun/all_to_all | solution.py:452
  46.7 0.9 %fusion.pick_ref = bf16[256,640]{1,0:T(8,128)(2,1)} fusion(s32[640]{0:T(1024)S(1)} %eq.19), kind=kLoop, calls=%fused_computation.1 | loop fusion | flops 327680 | bytes 330240 | tf_op jit(solution)/shard_map/cond/branch_0_fun/convert_element_type | solution.py:457
  48.0 20.2 %project.3 = (f32[256,1024]{1,0:T(8,128)}, f32[256,1024]{1,0:T(8,128)}) custom-call(s32[1]{0:T(128)} %get-tuple-element.74.me, bf16[8192,1024]{1,0:T(8,128)(2,1)} %get-tuple-element.146.gate_weight_ref, bf16[8192,1024]{1,0:T(8,128)(2,1)} %get-tuple-element.149.up_weight_ref, bf16[128,8192]{1,0:T(8,128)(2,1)} %get-tuple-element.70.own_ref, ...), custom_call_target="tpu_custom_call" | custom-call | flops 8589934592 | bytes 37748736 | tf_op jit(solution)/shard_map/cond/branch_0_fun/project/pallas_call | solution.py:345
  68.2 10.2 %all-to-all-done = bf16[8,80,1024]{2,1,0:T(8,128)(2,1)S(1)} async-done(((bf16[8,80,1024]{2,1,0:T(8,128)(2,1)}), bf16[8,80,1024]{2,1,0:T(8,128)(2,1)S(1)}, u32[]{:S(2)}, u32[]{:S(2)}) %all-to-all-start) | async-done | bytes 1310752 | tf_op jit(solution)/shard_map/cond/branch_0_fun/all_to_all | solution.py:452
  78.5 2.8 %combine.3 = bf16[256,1024]{1,0:T(8,128)(2,1)} custom-call(bf16[256,640]{1,0:T(8,128)(2,1)} %fusion.pick_ref, f32[256,1024]{1,0:T(8,128)} %get-tuple-element.78.gate_ref, f32[256,1024]{1,0:T(8,128)} %get-tuple-element.79.up_ref, bf16[640,1024]{1,0:T(8,128)(2,1)S(1)} %bitcast.13), custom_call_target="tpu_custom_call" | custom-call | flops 335544320 | bytes 2621440 | tf_op jit(solution)/shard_map/cond/branch_0_fun/combine/pallas_call | solution.py:378
  (23 shorter events, 1.5 us)
Async XLA Ops:
  0.0 37.2 %collective-permute-start.20 = (bf16[64,16384]{1,0:T(8,128)(2,1)}, bf16[64,16384]{1,0:T(8,128)(2,1)}, u32[]{:S(2)}, u32[]{:S(2)}) collective-permute-start(bf16[64,16384]{1,0:T(8,128)(2,1)} %bitcast.14), channel_id=1, source_target_pairs={{0,1},{1,0},{2,3},{3,2},{4,5},{5,4},{6,7},{7,6},{8,9},{9,8},{10,11... | collective-permute-start | bytes 6291464 | tf_op jit(solution)/shard_map/ppermute | solution.py:419
  0.5 5.8 %collective-permute-start.4 = (s32[16]{0:T(128)}, s32[16]{0:T(128)S(1)}, u32[]{:S(2)}, u32[]{:S(2)}) collective-permute-start(s32[16]{0:T(128)} %refs_0_), channel_id=1, source_target_pairs={{0,16},{16,0},{1,17},{17,1},{2,18},{18,2},{3,19},{19,3},{4,20},{20... | collective-permute-start | bytes 200 | tf_op jit(solution)/shard_map/ppermute | solution.py:428
  2.9 17.1 %collective-permute-start.3 = (bf16[64,8192]{1,0:T(8,128)(2,1)}, bf16[64,8192]{1,0:T(8,128)(2,1)S(1)}, u32[]{:S(2)}, u32[]{:S(2)}) collective-permute-start(bf16[64,8192]{1,0:T(8,128)(2,1)} %bitcast.18), channel_id=1, source_target_pairs={{0,1},{1,0},{2,3},{3,2},{4,5},{5,4},{6,7},{7,6},{8,9},{9,8},{10,11... | collective-permute-start | bytes 3145736 | tf_op jit(solution)/shard_map/ppermute | solution.py:419
  4.2 5.7 %collective-permute-start.7 = (bf16[16,4096]{1,0:T(8,128)(2,1)S(1)}, bf16[16,4096]{1,0:T(8,128)(2,1)S(1)}, u32[]{:S(2)}, u32[]{:S(2)}) collective-permute-start(bf16[16,4096]{1,0:T(8,128)(2,1)S(1)} %get-tuple-element.152), channel_id=1, source_target_pairs={{0,4},{1,5},{4,8},{5,9},{8,12},{9,13},{12,14},{13,15},{14,10},{15,... | collective-permute-start | bytes 393224 | tf_op jit(solution)/shard_map/ppermute | solution.py:39
  5.8 6.4 %collective-permute-start.8 = (bf16[16,4096]{1,0:T(8,128)(2,1)S(1)}, bf16[16,4096]{1,0:T(8,128)(2,1)S(1)}, u32[]{:S(2)}, u32[]{:S(2)}) collective-permute-start(bf16[16,4096]{1,0:T(8,128)(2,1)S(1)} %get-tuple-element.153), channel_id=1, source_target_pairs={{0,2},{1,3},{4,0},{5,1},{8,4},{9,5},{12,8},{13,9},{14,12},{15,13},... | collective-permute-start | bytes 393224 | tf_op jit(solution)/shard_map/ppermute | solution.py:39
  6.2 8.4 %collective-permute-start.6 = (bf16[16,4096]{1,0:T(8,128)(2,1)S(1)}, bf16[16,4096]{1,0:T(8,128)(2,1)S(1)}, u32[]{:S(2)}, u32[]{:S(2)}) collective-permute-start(bf16[16,4096]{1,0:T(8,128)(2,1)S(1)} %get-tuple-element.152), channel_id=1, source_target_pairs={{0,2},{1,3},{4,0},{5,1},{8,4},{9,5},{12,8},{13,9},{14,12},{15,13},... | collective-permute-start | bytes 393224 | tf_op jit(solution)/shard_map/ppermute | solution.py:39
  9.9 6.4 %collective-permute-start.9 = (bf16[16,4096]{1,0:T(8,128)(2,1)S(1)}, bf16[16,4096]{1,0:T(8,128)(2,1)S(1)}, u32[]{:S(2)}, u32[]{:S(2)}) collective-permute-start(bf16[16,4096]{1,0:T(8,128)(2,1)S(1)} %collective-permute-done.7.refs_6_), channel_id=1, source_target_pairs={{0,4},{1,5},{4,8},{5,9},{8,12},{9,13},{12,14},{13,15},{14,10},{15,... | collective-permute-start | bytes 393224 | tf_op jit(solution)/shard_map/ppermute | solution.py:39
  12.2 5.7 %collective-permute-start.10 = (bf16[16,4096]{1,0:T(8,128)(2,1)S(1)}, bf16[16,4096]{1,0:T(8,128)(2,1)S(1)}, u32[]{:S(2)}, u32[]{:S(2)}) collective-permute-start(bf16[16,4096]{1,0:T(8,128)(2,1)S(1)} %collective-permute-done.8.refs_7_), channel_id=1, source_target_pairs={{0,2},{1,3},{4,0},{5,1},{8,4},{9,5},{12,8},{13,9},{14,12},{15,13},... | collective-permute-start | bytes 393224 | tf_op jit(solution)/shard_map/ppermute | solution.py:39
  14.7 5.3 %collective-permute-start.5 = (bf16[16,4096]{1,0:T(8,128)(2,1)S(1)}, bf16[16,4096]{1,0:T(8,128)(2,1)S(1)}, u32[]{:S(2)}, u32[]{:S(2)}) collective-permute-start(bf16[16,4096]{1,0:T(8,128)(2,1)S(1)} %get-tuple-element.153), channel_id=1, source_target_pairs={{0,4},{1,5},{4,8},{5,9},{8,12},{9,13},{12,14},{13,15},{14,10},{15,... | collective-permute-start | bytes 393224 | tf_op jit(solution)/shard_map/ppermute | solution.py:39
  16.3 6.6 %collective-permute-start.13 = (bf16[16,4096]{1,0:T(8,128)(2,1)S(1)}, bf16[16,4096]{1,0:T(8,128)(2,1)S(1)}, u32[]{:S(2)}, u32[]{:S(2)}) collective-permute-start(bf16[16,4096]{1,0:T(8,128)(2,1)S(1)} %collective-permute-done.9.refs_10_), channel_id=1, source_target_pairs={{0,4},{1,5},{4,8},{5,9},{8,12},{9,13},{12,14},{13,15},{14,10},{15,... | collective-permute-start | bytes 393224 | tf_op jit(solution)/shard_map/ppermute | solution.py:39
  17.8 6.6 %collective-permute-start.14 = (bf16[16,4096]{1,0:T(8,128)(2,1)S(1)}, bf16[16,4096]{1,0:T(8,128)(2,1)S(1)}, u32[]{:S(2)}, u32[]{:S(2)}) collective-permute-start(bf16[16,4096]{1,0:T(8,128)(2,1)S(1)} %collective-permute-done.10.refs_11_), channel_id=1, source_target_pairs={{0,2},{1,3},{4,0},{5,1},{8,4},{9,5},{12,8},{13,9},{14,12},{15,13},... | collective-permute-start | bytes 393224 | tf_op jit(solution)/shard_map/ppermute | solution.py:39
  20.0 7.7 %copy-start = (bf16[64,8192]{1,0:T(8,128)(2,1)}, bf16[64,8192]{1,0:T(8,128)(2,1)S(1)}, u32[]{:S(2)}) copy-start(bf16[64,8192]{1,0:T(8,128)(2,1)S(1)} %collective-permute-done.3.refs_4_.other_down_ref) | copy-start | bytes 3145732
  20.0 5.7 %collective-permute-start.11 = (bf16[16,4096]{1,0:T(8,128)(2,1)S(1)}, bf16[16,4096]{1,0:T(8,128)(2,1)S(1)}, u32[]{:S(2)}, u32[]{:S(2)}) collective-permute-start(bf16[16,4096]{1,0:T(8,128)(2,1)S(1)} %collective-permute-done.5.refs_8_), channel_id=1, source_target_pairs={{0,4},{1,5},{4,8},{5,9},{8,12},{9,13},{12,14},{13,15},{14,10},{15,... | collective-permute-start | bytes 393224 | tf_op jit(solution)/shard_map/ppermute | solution.py:39
  21.6 5.7 %collective-permute-start.12 = (bf16[16,4096]{1,0:T(8,128)(2,1)S(1)}, bf16[16,4096]{1,0:T(8,128)(2,1)S(1)}, u32[]{:S(2)}, u32[]{:S(2)}) collective-permute-start(bf16[16,4096]{1,0:T(8,128)(2,1)S(1)} %collective-permute-done.6.refs_9_), channel_id=1, source_target_pairs={{0,2},{1,3},{4,0},{5,1},{8,4},{9,5},{12,8},{13,9},{14,12},{15,13},... | collective-permute-start | bytes 393224 | tf_op jit(solution)/shard_map/ppermute | solution.py:39
  22.8 9.9 %collective-permute-start.17 = (bf16[16,4096]{1,0:T(8,128)(2,1)S(1)}, bf16[16,4096]{1,0:T(8,128)(2,1)S(1)}, u32[]{:S(2)}, u32[]{:S(2)}) collective-permute-start(bf16[16,4096]{1,0:T(8,128)(2,1)S(1)} %collective-permute-done.13.refs_0_), channel_id=1, source_target_pairs={{0,4},{1,5},{4,8},{5,9},{8,12},{9,13},{12,14},{13,15},{14,10},{15,... | collective-permute-start | bytes 393224 | tf_op jit(solution)/shard_map/ppermute | solution.py:39
  24.4 8.3 %collective-permute-start.18 = (bf16[16,4096]{1,0:T(8,128)(2,1)S(1)}, bf16[16,4096]{1,0:T(8,128)(2,1)S(1)}, u32[]{:S(2)}, u32[]{:S(2)}) collective-permute-start(bf16[16,4096]{1,0:T(8,128)(2,1)S(1)} %collective-permute-done.14.refs_1_), channel_id=1, source_target_pairs={{0,2},{1,3},{4,0},{5,1},{8,4},{9,5},{12,8},{13,9},{14,12},{15,13},... | collective-permute-start | bytes 393224 | tf_op jit(solution)/shard_map/ppermute | solution.py:39
  25.7 7.0 %collective-permute-start.15 = (bf16[16,4096]{1,0:T(8,128)(2,1)S(1)}, bf16[16,4096]{1,0:T(8,128)(2,1)S(1)}, u32[]{:S(2)}, u32[]{:S(2)}) collective-permute-start(bf16[16,4096]{1,0:T(8,128)(2,1)S(1)} %collective-permute-done.11.refs_12_), channel_id=1, source_target_pairs={{0,4},{1,5},{4,8},{5,9},{8,12},{9,13},{12,14},{13,15},{14,10},{15,... | collective-permute-start | bytes 393224 | tf_op jit(solution)/shard_map/ppermute | solution.py:39
  27.3 5.5 %collective-permute-start.16 = (bf16[16,4096]{1,0:T(8,128)(2,1)S(1)}, bf16[16,4096]{1,0:T(8,128)(2,1)S(1)}, u32[]{:S(2)}, u32[]{:S(2)}) collective-permute-start(bf16[16,4096]{1,0:T(8,128)(2,1)S(1)} %collective-permute-done.12.refs_13_), channel_id=1, source_target_pairs={{0,2},{1,3},{4,0},{5,1},{8,4},{9,5},{12,8},{13,9},{14,12},{15,13},... | collective-permute-start | bytes 393224 | tf_op jit(solution)/shard_map/ppermute | solution.py:39
  32.7 4.5 %copy-start.3 = (s32[16]{0:T(128)S(1)}, s32[16]{0:T(128)}, u32[]{:S(2)}) copy-start(s32[16]{0:T(128)} %refs_0_) | copy-start | bytes 196
  35.9 1.3 %collective-permute-start.19 = (bf16[128,128]{1,0:T(8,128)(2,1)S(1)}, bf16[128,128]{1,0:T(8,128)(2,1)S(1)}, u32[]{:S(2)}, u32[]{:S(2)}) collective-permute-start(bf16[128,128]{1,0:T(8,128)(2,1)S(1)} %get-tuple-element.138), channel_id=1, source_target_pairs={{0,1},{1,0},{2,3},{3,2},{4,5},{5,4},{6,7},{7,6},{8,9},{9,8},{10,11... | collective-permute-start | bytes 98312 | tf_op jit(solution)/shard_map/ppermute | solution.py:419
  37.2 9.4 %collective-permute-start = (bf16[128,8192]{1,0:T(8,128)(2,1)}, bf16[128,8192]{1,0:T(8,128)(2,1)S(1)}, u32[]{:S(2)}, u32[]{:S(2)}) collective-permute-start(bf16[128,8192]{1,0:T(8,128)(2,1)} %get-tuple-element.70.own_ref), channel_id=1, source_target_pairs={{0,1},{1,0},{2,3},{3,2},{4,5},{5,4},{6,7},{7,6},{8,9},{9,8},{10,11... | collective-permute-start | bytes 6291464 | tf_op jit(solution)/shard_map/cond/branch_0_fun/ppermute | solution.py:419
  41.4 37.1 %all-to-all-start = ((bf16[8,80,1024]{2,1,0:T(8,128)(2,1)}), bf16[8,80,1024]{2,1,0:T(8,128)(2,1)S(1)}, u32[]{:S(2)}, u32[]{:S(2)}) async-start(bf16[8,80,1024]{2,1,0:T(8,128)(2,1)} %expand.3), calls=%async_computation | async-start | bytes 2621440 | tf_op jit(solution)/shard_map/cond/branch_0_fun/all_to_all | solution.py:452
  46.6 1.4 %copy-start.1 = (bf16[128,8192]{1,0:T(8,128)(2,1)}, bf16[128,8192]{1,0:T(8,128)(2,1)S(1)}, u32[]{:S(2)}) copy-start(bf16[128,8192]{1,0:T(8,128)(2,1)S(1)} %collective-permute-done.other_ref) | copy-start | bytes 6291460 | tf_op jit(solution)/shard_map/cond
